TPU v7x, 32 devices: a whole 2x2x4 slice. The times are simulated.
32 devices in a mesh: grp: 1, kz: 32 (over z, y, x, core).
Axes of the slice: x: 2, y: 2, z: 4, core: 2. Of those that a mesh axis runs over, the one named last changes fastest.
Arguments:
- kspace: float32 [8, 16, 512, 512], P('grp', None, 'kz'), may hold values from -8 to 8
- sensitivity: float32 [2, 256, 8, 16, 512], P(None, ('grp', 'kz')), may hold values from -2 to 2
- weight_first: bfloat16 [24, 2, 3, 3, 3], replicated, may hold values from -0.875 to 0.875
- bias_first: float32 [24], replicated, may hold values from -0.5 to 0.5
- weight_second: bfloat16 [24, 24, 3, 3, 3], replicated, may hold values from -0.3125 to 0.3125
- bias_second: float32 [24], replicated, may hold values from -0.5 to 0.5
- weight_third: bfloat16 [24, 24, 3, 3, 3], replicated, may hold values from -0.3125 to 0.3125
- bias_third: float32 [24], replicated, may hold values from -0.5 to 0.5
Outputs:
- features: bfloat16 [24, 512, 16, 256], P('grp', 'kz')
All inputs are finite; a program needn't handle non-finite values.
Results may differ from a plain program's by a relative error of at most 0.0058.
Values may be sent and summed in bfloat16 or wider, within the bound.
No kernel may reach another device: no remote copies, remote signals or barrier semaphores. Data moves between devices by JAX's collectives and lax.ppermute only.
A program may use at most 192 MiB of HBM per device.

v0:
```python
import math
import jax
import jax.numpy as jnp
from jax import lax
from jax.sharding import PartitionSpec as P

HIGHEST_PRECISION = lax.Precision.HIGHEST


def padded(x, sides, width):
    for axis, dim in sides:
        peers, length = (lax.axis_size(axis), x.shape[dim])
        up = [(i, (i + 1) % peers) for i in range(peers - 1)]
        down = [(j, i) for i, j in up]
        last = lax.slice_in_dim(x, length - width, length, axis=dim)
        first = lax.slice_in_dim(x, 0, width, axis=dim)
        before = lax.ppermute(last, axis, up)
        after = lax.ppermute(first, axis, down)
        x = jnp.concatenate([before, x, after], axis=dim)
    return x


def dft_parts(length):
    positions = jnp.arange(length, dtype=jnp.int32)
    phase_int = positions[:, None] * positions[None, :] % length
    angles = phase_int.astype(jnp.float32) * (2.0 * math.pi / length)
    factor = 1.0 / math.sqrt(length)
    return (jnp.cos(angles) * factor, jnp.sin(angles) * factor)


def y_table(length):
    cosine, sine_part = dft_parts(length)
    upper = jnp.concatenate([cosine, sine_part], axis=1)
    lower = jnp.concatenate([-sine_part, cosine], axis=1)
    return jnp.concatenate([upper, lower], axis=0)


def z_stacked(length):
    cosine, sine_part = dft_parts(length)
    from_real = jnp.stack([cosine, sine_part], axis=1)
    from_imag = jnp.stack([-sine_part, cosine], axis=1)
    return jnp.stack([from_real, from_imag], axis=1).reshape(2 * length, 2 * length)


def convolve(volume, weight, bias_vec):
    result = lax.conv_general_dilated(
        volume[None],
        weight,
        (1, 1, 1),
        [(0, 0), (1, 1), (1, 1)],
        dimension_numbers=("NCDHW", "OIDHW", "NCDHW"),
        preferred_element_type=jnp.float32,
    )[0]
    return jnp.maximum(result + bias_vec[:, None, None, None], 0.0)


def on_device(
    kspace,
    sensitivity,
    weight_first,
    bias_first,
    weight_second,
    bias_second,
    weight_third,
    bias_third,
):
    coil_count, rows_x, kz_local, twice_y = kspace.shape
    y_count = twice_y // 2
    kz_count = kz_local * lax.axis_size("kz")
    flat = kspace.reshape(-1, twice_y)
    y_lines = jnp.dot(
        flat, y_table(y_count), precision=HIGHEST_PRECISION, preferred_element_type=jnp.float32
    )
    y_lines = y_lines.reshape(coil_count, rows_x, kz_local, 2, y_count)
    z_matrix = z_stacked(kz_count)
    pieces = lax.all_to_all(y_lines, "kz", split_axis=4, concat_axis=2, tiled=True)
    coils_here, rows_here, kz_all, parts_here, y_here = pieces.shape
    grouped = pieces.reshape(coils_here * rows_here, kz_all * parts_here, y_here)
    product = lax.dot_general(
        grouped,
        z_matrix,
        (((1,), (0,)), ((), ())),
        precision=HIGHEST_PRECISION,
        preferred_element_type=jnp.float32,
    )
    coil_images = product.reshape(coils_here, rows_here, y_here, 2, kz_all)
    sens_view = jnp.transpose(sensitivity, (0, 2, 3, 1, 4))
    sens_re = sens_view[0]
    sens_im = sens_view[1]
    coil_re = coil_images[:, :, :, 0]
    coil_im = coil_images[:, :, :, 1]
    merged_re = jnp.sum(sens_re * coil_re + sens_im * coil_im, axis=0)
    merged_im = jnp.sum(sens_re * coil_im - sens_im * coil_re, axis=0)
    merged = jnp.stack([merged_re, merged_im], axis=0).astype(jnp.bfloat16)
    gathered = lax.all_to_all(merged, "kz", split_axis=3, concat_axis=2, tiled=True)
    slices = jnp.transpose(gathered, (0, 3, 1, 2))
    layers = ((weight_first, bias_first), (weight_second, bias_second), (weight_third, bias_third))
    activity = slices
    for weight, bias_vec in layers:
        extended = padded(activity, (("kz", 1),), 1)
        activity = convolve(extended, weight, bias_vec).astype(jnp.bfloat16)
    return activity


def solution(mesh):
    in_specs = (
        P("grp", None, "kz", None),
        P(None, ("grp", "kz"), None, None, None),
        P(),
        P(),
        P(),
        P(),
        P(),
        P(),
    )
    out_specs = P("grp", "kz", None, None)
    return jax.shard_map(
        on_device, mesh=mesh, in_specs=in_specs, out_specs=out_specs, check_vma=False
    )
```

profile of v0, /device:TPU:7, one launch (start us, length us, event | category | flops | bytes accessed | tf_op | source)
XLA Modules:
  0.0 860.8 jit_solution(986464142390691730)
XLA Ops:
  2.0 16.8 %convolution_bitcast_fusion = f32[2048,512]{0,1:T(8,128)} fusion(f32[2048,512]{1,0:T(8,128)} %bitcast.175, f32[256,256]{1,0:T(8,128)S(1)} %get-tuple-element.16, f32[256,256]{1,0:T(8,128)S(1)} %fusion.55, f32[256,256]{1,0:T(8,128)S(1)} %get-tuple-element.15), kind=kOutput, calls=%fused_computation.39 | convolution fusion | flops 6443237376 | bytes 9175040 | tf_op jit(solution)/shard_map/dot_general | solution.py:71
  30.1 26.3 %copy.113 = f32[8,16,16,2,256]{2,1,3,0,4:T(8,128)} copy(f32[8,16,16,2,256]{4,3,2,1,0:T(2,128)} %reshape.101) | data formatting | bytes 8388608 | tf_op jit(solution)/shard_map/reshape | solution.py:74
  56.4 29.0 %reshape.144 = f32[32,1,32768]{2,1,0:T(1,128)} reshape(f32[256,8,2,16,16]{4,3,2,1,0:T(8,128)} %bitcast.163) | data formatting | bytes 8388608
  120.8 64.2 %all-to-all-done = f32[32,1,32768]{2,1,0:T(1,128)} async-done(((f32[32,1,32768]{2,1,0:T(1,128)}), f32[32,1,32768]{2,1,0:T(1,128)}, u32[]{:S(2)}, u32[]{:S(2)}) %all-to-all-start) | async-done | bytes 4194336 | tf_op jit(solution)/shard_map/all_to_all | solution.py:76
  185.5 14.5 %reduce = f32[32,32768]{1,0:T(8,128)} reduce(f32[32,1,32768]{2,1,0:T(1,128)} %all-to-all-done, f32[]{:T(128)} %broadcast.231), dimensions={1}, to_apply=%all_to_all.24.reduce_sub_computation | reduce | bytes 8388612 | tf_op jit(solution)/shard_map/all_to_all | solution.py:76
  200.0 28.9 %reshape.145 = f32[256,8,2,16,16]{4,3,2,1,0:T(8,128)} reshape(f32[32,32768]{1,0:T(8,128)} %reduce) | data formatting | bytes 8388608
  228.9 36.6 %copy.115 = f32[8,16,32,16,2,8]{1,0,5,4,3,2:T(8,128)} copy(f32[8,16,32,16,2,8]{3,1,4,0,5,2:T(8,128)} %bitcast.164) | data formatting | bytes 8388608 | tf_op jit(solution)/shard_map/all_to_all | solution.py:76
  265.5 21.4 %reshape.102 = f32[128,1024,8]{0,2,1:T(8,128)} reshape(f32[8,16,32,16,2,8]{1,0,5,4,3,2:T(8,128)} %copy.115) | data formatting | bytes 8388608 | tf_op jit(solution)/shard_map/reshape | solution.py:78
  292.5 16.8 %fusion.69 = f32[8,16,8,2,512]{4,2,3,1,0:T(8,128)S(1)} fusion(f32[8,16,8,1024,1]{3,2,4,1,0:T(8,128)} %bitcast.174, f32[2,512,1024,1,1]{2,1,0,4,3:T(8,128)} %bitcast.173), kind=kOutput, calls=%fused_computation.97 | convolution fusion | flops 12884901888 | bytes 12582912 | tf_op jit(solution)/shard_map/dot_general | solution.py:79
  314.8 13.3 %all_to_all.33 = bf16[32,2,2048]{2,1,0:T(2,128)(2,1)S(1)} all-to-all(bf16[32,2,2048]{2,1,0:T(2,128)(2,1)S(1)} %reshape.146), channel_id=1, replica_groups=mesh['grp'=1,'kz'=32] {'kz'}, dimensions={0} | all-to-all | bytes 524288 | tf_op jit(solution)/shard_map/all_to_all | solution.py:95
  364.1 15.1 %fusion.82 = bf16[2,18,16,8,35]{3,0,4,2,1:T(2,128)(2,1)S(1)} fusion(bf16[2,18,16,1,7,2]{4,0,5,2,1,3:T(2,128)(2,1)S(1)} %slice.52, bf16[2,18,16,1,8,33]{4,0,5,2,1,3:T(2,128)(2,1)} %copy.127), kind=kLoop, calls=%fused_computation.34.clone.clone.1 | loop fusion | flops 967680 | bytes 642816 | tf_op jit(solution)/shard_map/conv_general_dilated | solution.py:46
  379.3 55.2 %convolution_select_fusion = f32[16,16,8,33,24]{4,2,3,1,0:T(8,128)} fusion(bf16[24,2,3,3,3]{0,1,4,3,2:T(2,128)(2,1)S(1)} %copy-done.7, pred[8,33]{0,1:T(8,128)(4,1)S(1)} %copy-done.8, bf16[2,18,16,8,35]{3,0,4,2,1:T(2,128)(2,1)S(1)} %fusion.82), kind=kOutput, calls=%fused_computation.16 | convolution fusion | flops 169500672 | bytes 6813480 | tf_op jit(solution)/shard_map/conv_general_dilated | solution.py:46
  434.5 32.2 %copy.128 = f32[16,16,8,33,24]{3,2,4,1,0:T(8,128)} copy(f32[16,16,8,33,24]{4,2,3,1,0:T(8,128)} %convolution_select_fusion) | data formatting | bytes 12976128 | tf_op jit(solution)/shard_map/conv_general_dilated | solution.py:46
  466.7 20.1 %reshape.110 = f32[16,16,1,264,24]{3,4,1,0,2:T(8,128)} reshape(f32[16,16,8,33,24]{3,2,4,1,0:T(8,128)} %copy.128) | data formatting | bytes 12976128 | tf_op jit(solution)/shard_map/conv_general_dilated | solution.py:46
  506.5 19.1 %reshape.142 = bf16[24,18,16,1,8,33]{5,4,0,2,1,3:T(8,128)(2,1)} reshape(bf16[24,18,16,1,264]{4,0,2,1,3:T(8,128)(2,1)} %pad.2) | data formatting | bytes 7299072 | tf_op jit(solution)/shard_map/conv_general_dilated | solution.py:46
  525.6 27.5 %copy.131 = bf16[24,18,16,1,8,33]{0,4,5,2,1,3:T(8,128)(2,1)} copy(bf16[24,18,16,1,8,33]{5,4,0,2,1,3:T(8,128)(2,1)} %reshape.142) | data formatting | bytes 7299072 | tf_op jit(solution)/shard_map/conv_general_dilated | solution.py:46
  554.8 63.6 %broadcast_select_fusion.1 = f32[16,16,8,33,24]{4,2,3,1,0:T(8,128)} fusion(pred[8,33]{0,1:T(8,128)(4,1)S(1)} %copy-done.8, bf16[24,24,3,3,3]{1,0,4,3,2:T(8,128)(2,1)S(1)} %copy-done, bf16[24,18,16,1,7,2]{0,4,5,2,1,3:T(8,128)(2,1)S(1)} %slice.56, bf16[24,18,16,1,8,33]{0,4,5,2,1,3:T(8,128)(2,1)} %copy.131), kind=kOutput, calls=%fused_computation.18 | convolution fusion | flops 2027778048 | bytes 10362504 | tf_op jit(solution)/shard_map/conv_general_dilated | solution.py:46
  618.3 32.0 %copy.132 = f32[16,16,8,33,24]{3,2,4,1,0:T(8,128)} copy(f32[16,16,8,33,24]{4,2,3,1,0:T(8,128)} %broadcast_select_fusion.1) | data formatting | bytes 12976128 | tf_op jit(solution)/shard_map/conv_general_dilated | solution.py:46
  650.4 20.1 %reshape.117 = f32[16,16,1,264,24]{3,4,1,0,2:T(8,128)} reshape(f32[16,16,8,33,24]{3,2,4,1,0:T(8,128)} %copy.132) | data formatting | bytes 12976128 | tf_op jit(solution)/shard_map/conv_general_dilated | solution.py:46
  690.4 19.1 %reshape.143 = bf16[24,18,16,1,8,33]{5,4,0,2,1,3:T(8,128)(2,1)} reshape(bf16[24,18,16,1,264]{4,0,2,1,3:T(8,128)(2,1)} %pad.4) | data formatting | bytes 7299072 | tf_op jit(solution)/shard_map/conv_general_dilated | solution.py:46
  709.5 27.5 %copy.135 = bf16[24,18,16,1,8,33]{0,4,5,2,1,3:T(8,128)(2,1)} copy(bf16[24,18,16,1,8,33]{5,4,0,2,1,3:T(8,128)(2,1)} %reshape.143) | data formatting | bytes 7299072 | tf_op jit(solution)/shard_map/conv_general_dilated | solution.py:46
  738.7 63.5 %broadcast_select_fusion = f32[16,16,8,33,24]{4,2,3,1,0:T(8,128)} fusion(pred[8,33]{0,1:T(8,128)(4,1)S(1)} %copy-done.8, bf16[24,24,3,3,3]{1,0,4,3,2:T(8,128)(2,1)S(1)} %copy-done.6, bf16[24,18,16,1,7,2]{0,4,5,2,1,3:T(8,128)(2,1)S(1)} %slice.60, bf16[24,18,16,1,8,33]{0,4,5,2,1,3:T(8,128)(2,1)} %copy.135), kind=kOutput, calls=%fused_computation.17 | convolution fusion | flops 2027778048 | bytes 10362504 | tf_op jit(solution)/shard_map/conv_general_dilated | solution.py:46
  802.2 32.0 %copy.136 = f32[16,16,8,33,24]{3,2,4,1,0:T(8,128)} copy(f32[16,16,8,33,24]{4,2,3,1,0:T(8,128)} %broadcast_select_fusion) | data formatting | bytes 12976128 | tf_op jit(solution)/shard_map/conv_general_dilated | solution.py:46
  834.3 20.1 %reshape.124 = f32[16,16,1,264,24]{3,4,1,0,2:T(8,128)} reshape(f32[16,16,8,33,24]{3,2,4,1,0:T(8,128)} %copy.136) | data formatting | bytes 12976128 | tf_op jit(solution)/shard_map/conv_general_dilated | solution.py:46
  (72 shorter events, 145.0 us)
Async XLA Ops:
  0.0 554.8 %copy-start = (bf16[24,24,3,3,3]{1,0,4,3,2:T(8,128)(2,1)S(1)}, bf16[24,24,3,3,3]{1,0,4,3,2:T(8,128)(2,1)}, u32[]{:S(2)}) copy-start(bf16[24,24,3,3,3]{1,0,4,3,2:T(8,128)(2,1)} %param.12) | copy-start | bytes 93316
  85.4 99.6 %all-to-all-start = ((f32[32,1,32768]{2,1,0:T(1,128)}), f32[32,1,32768]{2,1,0:T(1,128)}, u32[]{:S(2)}, u32[]{:S(2)}) async-start(f32[32,1,32768]{2,1,0:T(1,128)} %reshape.144), calls=%async_computation | async-start | bytes 8388608 | tf_op jit(solution)/shard_map/all_to_all | solution.py:76
  292.5 16.8 %copy-start.2 = (f32[2,8,8,16,512]{4,1,3,2,0:T(8,128)S(1)}, f32[2,8,8,16,512]{4,1,3,2,0:T(8,128)}, u32[]{:S(2)}) copy-start(f32[2,8,8,16,512]{4,1,3,2,0:T(8,128)} %copy.150) | copy-start | bytes 12582916
  339.3 9.2 %collective-permute-start = (bf16[2,1,16,256]{3,2,1,0:T(8,128)(2,1)S(1)}, bf16[2,1,16,256]{3,2,1,0:T(8,128)(2,1)S(1)}, u32[]{:S(2)}, u32[]{:S(2)}) collective-permute-start(bf16[2,1,16,256]{3,2,1,0:T(8,128)(2,1)S(1)} %copy.123), channel_id=1, source_target_pairs={{0,1},{1,2},{2,3},{3,4},{4,5},{5,6},{6,7},{7,8},{8,9},{9,10},{10,1... | collective-permute-start | bytes 49160 | tf_op jit(solution)/shard_map/ppermute | solution.py:17
  345.6 6.9 collective-permute-start.1
  364.1 15.1 %copy-start.7 = (bf16[24,2,3,3,3]{0,1,4,3,2:T(2,128)(2,1)S(1)}, bf16[24,2,3,3,3]{0,1,4,3,2:T(2,128)(2,1)}, u32[]{:S(2)}) copy-start(bf16[24,2,3,3,3]{0,1,4,3,2:T(2,128)(2,1)} %param.10) | copy-start | bytes 7780
  364.1 15.1 %copy-start.8 = (pred[8,33]{0,1:T(8,128)(4,1)S(1)}, pred[8,33]{0,1:T(8,128)(4,1)}, u32[]{:S(2)}) copy-start(pred[8,33]{0,1:T(8,128)(4,1)} %constant.54) | copy-start | bytes 796
  466.7 20.1 %copy-start.3 = (f32[24]{0:T(128)S(1)}, f32[24]{0:T(128)}, u32[]{:S(2)}) copy-start(f32[24]{0:T(128)} %param.11) | copy-start | bytes 292
  490.5 4.5 collective-permute-start.2
  492.4 8.8 %collective-permute-start.3 = (bf16[24,1,16,256]{3,0,2,1:T(8,128)(2,1)S(1)}, bf16[24,1,16,256]{3,0,2,1:T(8,128)(2,1)S(1)}, u32[]{:S(2)}, u32[]{:S(2)}) collective-permute-start(bf16[24,1,16,256]{3,0,2,1:T(8,128)(2,1)S(1)} %get-tuple-element.10), channel_id=1, source_target_pairs={{1,0},{2,1},{3,2},{4,3},{5,4},{6,5},{7,6},{8,7},{9,8},{10,9},{11,1... | collective-permute-start | bytes 589832 | tf_op jit(solution)/shard_map/ppermute | solution.py:18
  650.4 20.1 %copy-start.4 = (f32[24]{0:T(128)S(1)}, f32[24]{0:T(128)}, u32[]{:S(2)}) copy-start(f32[24]{0:T(128)} %param.13) | copy-start | bytes 292
  674.1 4.5 collective-permute-start.4
  676.1 8.8 %collective-permute-start.5 = (bf16[24,1,16,256]{3,0,2,1:T(8,128)(2,1)S(1)}, bf16[24,1,16,256]{3,0,2,1:T(8,128)(2,1)S(1)}, u32[]{:S(2)}, u32[]{:S(2)}) collective-permute-start(bf16[24,1,16,256]{3,0,2,1:T(8,128)(2,1)S(1)} %get-tuple-element.8), channel_id=1, source_target_pairs={{1,0},{2,1},{3,2},{4,3},{5,4},{6,5},{7,6},{8,7},{9,8},{10,9},{11,1... | collective-permute-start | bytes 589832 | tf_op jit(solution)/shard_map/ppermute | solution.py:18
  709.5 29.2 %copy-start.6 = (bf16[24,24,3,3,3]{1,0,4,3,2:T(8,128)(2,1)S(1)}, bf16[24,24,3,3,3]{1,0,4,3,2:T(8,128)(2,1)}, u32[]{:S(2)}) copy-start(bf16[24,24,3,3,3]{1,0,4,3,2:T(8,128)(2,1)} %param.14) | copy-start | bytes 93316
  834.3 20.1 %copy-start.5 = (f32[24]{0:T(128)S(1)}, f32[24]{0:T(128)}, u32[]{:S(2)}) copy-start(f32[24]{0:T(128)} %param.15) | copy-start | bytes 292
  854.4 6.0 copy-start.1
where the time goes:
time: 877 us; the launch traced here: 861 us
  local copies, waits for them, and re-layouts  475 us (54%)
  matrix products  216 us (25%)
  waiting for transfers between devices  81 us (9%)
  other arithmetic  53.8 us (6%)
  starting transfers between devices  21.6 us (2%)
  blocking collectives  13.3 us (2%)
    conv_general_dilated x15, local copies, waits for them, and re-layouts, convolve(): lax.conv_general_dilated(volume[None], weight, (1, 1, 1), [(0, 0), (1, 1)...  265 us
    conv_general_dilated x3, matrix products, convolve(): lax.conv_general_dilated(volume[None], weight, (1, 1, 1), [(0, 0), (1, 1)...  182 us
    unnamed x24, local copies, waits for them, and re-layouts  73.1 us
    all_to_all x1, waiting for transfers between devices, on_device(): lax.all_to_all(y_lines, 'kz', split_axis=4, concat_axis=2, tiled=True)  64.2 us
    all_to_all x2, local copies, waits for them, and re-layouts, on_device(): lax.all_to_all(y_lines, 'kz', split_axis=4, concat_axis=2, tiled=True)  37.1 us
    reshape x2, local copies, waits for them, and re-layouts, on_device(): y_lines = y_lines.reshape(coil_count, rows_x, kz_local, 2, y_count)  32.2 us
    reshape x1, local copies, waits for them, and re-layouts, on_device(): pieces.reshape(coils_here * rows_here, kz_all * parts_here, y_here)  21.4 us
  transfers between devices with their start and end apart: 7, of which 6 were waited for; matrix products, arithmetic and copies ran while one was open for 4% of the time, Pallas kernels for 0%

commit v1 on v0

--- a/solution.py
+++ b/solution.py
@@ -73,7 +73,9 @@
     )
     y_lines = y_lines.reshape(coil_count, rows_x, kz_local, 2, y_count)
     z_matrix = z_stacked(kz_count)
-    pieces = lax.all_to_all(y_lines, "kz", split_axis=4, concat_axis=2, tiled=True)
+    shards = jnp.split(y_lines, lax.axis_size("kz"), axis=4)
+    received = lax.all_to_all(jnp.stack(shards), "kz", 0, 0)
+    pieces = jnp.concatenate(received, axis=2)
     coils_here, rows_here, kz_all, parts_here, y_here = pieces.shape
     grouped = pieces.reshape(coils_here * rows_here, kz_all * parts_here, y_here)
     product = lax.dot_general(

time: 877 us -> 1070 us (1.22)
  local copies, waits for them, and re-layouts: 475 us -> 670 us
    unnamed x24 -> x57, local copies, waits for them, and re-layouts: 73.1 us -> 185 us
    another operation x0 -> x3, local copies, waits for them, and re-layouts: none -> 108 us  [the longest x2 86.5 us: on_device(): received = lax.all_to_all(jnp.stack(shards), 'kz', 0, 0)]
    reshape x1 -> x2, local copies, waits for them, and re-layouts: 21.4 us -> 60 us  [on_device(): pieces = jnp.concatenate(received, axis=2)]
    all_to_all x2 -> x1, local copies, waits for them, and re-layouts: 37.1 us -> 0.51 us  [on_device(): received = lax.all_to_all(jnp.stack(shards), 'kz', 0, 0)]
    reshape x2 -> x1, local copies, waits for them, and re-layouts: 32.2 us -> 6.06 us  [on_device(): y_lines = y_lines.reshape(coil_count, rows_x, kz_local, 2, y_count)]
  transfers between devices with their start and end apart: 7 -> 7, of which waited for: 6 -> 6; matrix products, arithmetic and copies ran while one was open for 4% -> 3% of each run, Pallas kernels for 0% -> 0%
where the time goes in v1:
time: 1070 us; the launch traced here: 1060 us
  local copies, waits for them, and re-layouts  670 us (63%)
  matrix products  216 us (20%)
  waiting for transfers between devices  81 us (8%)
  other arithmetic  54 us (5%)
  starting transfers between devices  21.6 us (2%)
  blocking collectives  13.6 us (1%)
    conv_general_dilated x15, local copies, waits for them, and re-layouts, convolve(): lax.conv_general_dilated(volume[None], weight, (1, 1, 1), [(0, 0), (1, 1)...  265 us
    unnamed x57, local copies, waits for them, and re-layouts  185 us
    conv_general_dilated x3, matrix products, convolve(): lax.conv_general_dilated(volume[None], weight, (1, 1, 1), [(0, 0), (1, 1)...  182 us
    another operation x2, local copies, waits for them, and re-layouts, on_device(): received = lax.all_to_all(jnp.stack(shards), 'kz', 0, 0)  86.5 us
    all_to_all x1, waiting for transfers between devices, on_device(): received = lax.all_to_all(jnp.stack(shards), 'kz', 0, 0)  64.3 us
    reshape x2, local copies, waits for them, and re-layouts, on_device(): pieces = jnp.concatenate(received, axis=2)  60 us
    another operation x1, local copies, waits for them, and re-layouts, on_device(): pieces.reshape(coils_here * rows_here, kz_all * parts_here, y_here)  21.5 us
  transfers between devices with their start and end apart: 7, of which 6 were waited for; matrix products, arithmetic and copies ran while one was open for 3% of the time, Pallas kernels for 0%

profile of v1, /device:TPU:7, one launch (start us, length us, event | category | flops | bytes accessed | tf_op | source)
XLA Modules:
  0.0 1057.2 jit_solution(5250533626432726458)
XLA Ops:
  2.0 16.9 %convolution_bitcast_fusion = f32[2048,512]{0,1:T(8,128)} fusion(f32[2048,512]{1,0:T(8,128)} %bitcast.302, f32[256,256]{1,0:T(8,128)S(1)} %get-tuple-element.16, f32[256,256]{1,0:T(8,128)S(1)} %fusion.87, f32[256,256]{1,0:T(8,128)S(1)} %get-tuple-element.15), kind=kOutput, calls=%fused_computation.39 | convolution fusion | flops 6443237376 | bytes 9175040 | tf_op jit(solution)/shard_map/dot_general | solution.py:71
  145.7 83.0 %copy.152 = f32[32,8,16,16,2,8]{3,5,4,2,1,0:T(8,128)} copy(f32[32,8,16,16,2,8]{5,4,3,2,1,0:T(2,128)} %fusion.35) | data formatting | bytes 8388608 | tf_op jit(solution)/shard_map/stack | solution.py:77
  228.7 29.0 %reshape.143 = f32[32,1,32768]{2,1,0:T(1,128)} reshape(f32[32,8,16,2,8,16]{5,4,3,2,1,0:T(8,128)} %bitcast.291) | data formatting | bytes 8388608
  293.1 64.3 %all-to-all-done = f32[32,1,32768]{2,1,0:T(1,128)} async-done(((f32[32,1,32768]{2,1,0:T(1,128)}), f32[32,1,32768]{2,1,0:T(1,128)}, u32[]{:S(2)}, u32[]{:S(2)}) %all-to-all-start) | async-done | bytes 4194336 | tf_op jit(solution)/shard_map/all_to_all | solution.py:77
  357.9 14.4 %reduce = f32[32,32768]{1,0:T(8,128)} reduce(f32[32,1,32768]{2,1,0:T(1,128)} %all-to-all-done, f32[]{:T(128)} %broadcast.231), dimensions={1}, to_apply=%all_to_all.16.reduce_sub_computation | reduce | bytes 8388612 | tf_op jit(solution)/shard_map/all_to_all | solution.py:77
  372.3 28.9 %reshape.144 = f32[32,8,16,2,8,16]{5,4,3,2,1,0:T(8,128)} reshape(f32[32,32768]{1,0:T(8,128)} %reduce) | data formatting | bytes 8388608
  401.2 22.9 %bitcast_bitcast_fusion = f32[8,16,32,16,2,8]{3,5,4,1,0,2:T(8,128)} fusion(f32[32,8,16,2,8,16]{5,4,3,2,1,0:T(8,128)} %reshape.144), kind=kLoop, calls=%fused_computation.161 | loop fusion | bytes 8388608 | tf_op jit(solution)/shard_map/reshape | solution.py:78
  424.1 37.2 %copy.153 = f32[8,16,32,16,2,8]{1,0,5,4,3,2:T(8,128)} copy(f32[8,16,32,16,2,8]{3,5,4,1,0,2:T(8,128)} %bitcast_bitcast_fusion) | data formatting | bytes 8388608 | tf_op jit(solution)/shard_map/reshape | solution.py:78
  461.3 21.5 %reshape_reshape.3 = f32[128,1024,8]{0,2,1:T(8,128)} reshape(f32[8,16,32,16,2,8]{1,0,5,4,3,2:T(8,128)} %copy.153) | data formatting | bytes 8388608 | tf_op jit(solution)/shard_map/reshape;reshape | solution.py:80
  488.2 16.8 %fusion.101 = f32[8,16,8,2,512]{4,2,3,1,0:T(8,128)S(1)} fusion(f32[8,16,8,1024,1]{3,2,4,1,0:T(8,128)} %bitcast.301, f32[2,512,1024,1,1]{2,1,0,4,3:T(8,128)} %bitcast.300), kind=kOutput, calls=%fused_computation.162 | convolution fusion | flops 12884901888 | bytes 12582912 | tf_op jit(solution)/shard_map/dot_general | solution.py:81
  560.3 15.1 %fusion.114 = bf16[2,18,16,8,35]{3,0,4,2,1:T(2,128)(2,1)S(1)} fusion(bf16[2,18,16,1,7,2]{4,0,5,2,1,3:T(2,128)(2,1)S(1)} %slice.52, bf16[2,18,16,1,8,33]{4,0,5,2,1,3:T(2,128)(2,1)} %copy.165), kind=kLoop, calls=%fused_computation.34.clone.clone.1 | loop fusion | flops 967680 | bytes 642816 | tf_op jit(solution)/shard_map/conv_general_dilated | solution.py:46
  575.4 54.8 %convolution_select_fusion = f32[16,16,8,33,24]{4,2,3,1,0:T(8,128)} fusion(bf16[24,2,3,3,3]{0,1,4,3,2:T(2,128)(2,1)S(1)} %copy-done.8, pred[8,33]{0,1:T(8,128)(4,1)S(1)} %copy-done.9, bf16[2,18,16,8,35]{3,0,4,2,1:T(2,128)(2,1)S(1)} %fusion.114), kind=kOutput, calls=%fused_computation.16 | convolution fusion | flops 169500672 | bytes 6813480 | tf_op jit(solution)/shard_map/conv_general_dilated | solution.py:46
  630.3 32.2 %copy.166 = f32[16,16,8,33,24]{3,2,4,1,0:T(8,128)} copy(f32[16,16,8,33,24]{4,2,3,1,0:T(8,128)} %convolution_select_fusion) | data formatting | bytes 12976128 | tf_op jit(solution)/shard_map/conv_general_dilated | solution.py:46
  662.5 20.1 %reshape.109 = f32[16,16,1,264,24]{3,4,1,0,2:T(8,128)} reshape(f32[16,16,8,33,24]{3,2,4,1,0:T(8,128)} %copy.166) | data formatting | bytes 12976128 | tf_op jit(solution)/shard_map/conv_general_dilated | solution.py:46
  702.4 19.1 %reshape.141 = bf16[24,18,16,1,8,33]{5,4,0,2,1,3:T(8,128)(2,1)} reshape(bf16[24,18,16,1,264]{4,0,2,1,3:T(8,128)(2,1)} %pad.2) | data formatting | bytes 7299072 | tf_op jit(solution)/shard_map/conv_general_dilated | solution.py:46
  721.5 27.5 %copy.169 = bf16[24,18,16,1,8,33]{0,4,5,2,1,3:T(8,128)(2,1)} copy(bf16[24,18,16,1,8,33]{5,4,0,2,1,3:T(8,128)(2,1)} %reshape.141) | data formatting | bytes 7299072 | tf_op jit(solution)/shard_map/conv_general_dilated | solution.py:46
  750.7 63.7 %broadcast_select_fusion.1 = f32[16,16,8,33,24]{4,2,3,1,0:T(8,128)} fusion(pred[8,33]{0,1:T(8,128)(4,1)S(1)} %copy-done.9, bf16[24,24,3,3,3]{1,0,4,3,2:T(8,128)(2,1)S(1)} %copy-done, bf16[24,18,16,1,7,2]{0,4,5,2,1,3:T(8,128)(2,1)S(1)} %slice.56, bf16[24,18,16,1,8,33]{0,4,5,2,1,3:T(8,128)(2,1)} %copy.169), kind=kOutput, calls=%fused_computation.18 | convolution fusion | flops 2027778048 | bytes 10362504 | tf_op jit(solution)/shard_map/conv_general_dilated | solution.py:46
  814.4 32.0 %copy.170 = f32[16,16,8,33,24]{3,2,4,1,0:T(8,128)} copy(f32[16,16,8,33,24]{4,2,3,1,0:T(8,128)} %broadcast_select_fusion.1) | data formatting | bytes 12976128 | tf_op jit(solution)/shard_map/conv_general_dilated | solution.py:46
  846.4 20.1 %reshape.116 = f32[16,16,1,264,24]{3,4,1,0,2:T(8,128)} reshape(f32[16,16,8,33,24]{3,2,4,1,0:T(8,128)} %copy.170) | data formatting | bytes 12976128 | tf_op jit(solution)/shard_map/conv_general_dilated | solution.py:46
  886.6 19.1 %reshape.142 = bf16[24,18,16,1,8,33]{5,4,0,2,1,3:T(8,128)(2,1)} reshape(bf16[24,18,16,1,264]{4,0,2,1,3:T(8,128)(2,1)} %pad.4) | data formatting | bytes 7299072 | tf_op jit(solution)/shard_map/conv_general_dilated | solution.py:46
  905.7 27.5 %copy.173 = bf16[24,18,16,1,8,33]{0,4,5,2,1,3:T(8,128)(2,1)} copy(bf16[24,18,16,1,8,33]{5,4,0,2,1,3:T(8,128)(2,1)} %reshape.142) | data formatting | bytes 7299072 | tf_op jit(solution)/shard_map/conv_general_dilated | solution.py:46
  934.9 63.5 %broadcast_select_fusion = f32[16,16,8,33,24]{4,2,3,1,0:T(8,128)} fusion(pred[8,33]{0,1:T(8,128)(4,1)S(1)} %copy-done.9, bf16[24,24,3,3,3]{1,0,4,3,2:T(8,128)(2,1)S(1)} %copy-done.7, bf16[24,18,16,1,7,2]{0,4,5,2,1,3:T(8,128)(2,1)S(1)} %slice.60, bf16[24,18,16,1,8,33]{0,4,5,2,1,3:T(8,128)(2,1)} %copy.173), kind=kOutput, calls=%fused_computation.17 | convolution fusion | flops 2027778048 | bytes 10362504 | tf_op jit(solution)/shard_map/conv_general_dilated | solution.py:46
  998.4 32.0 %copy.174 = f32[16,16,8,33,24]{3,2,4,1,0:T(8,128)} copy(f32[16,16,8,33,24]{4,2,3,1,0:T(8,128)} %broadcast_select_fusion) | data formatting | bytes 12976128 | tf_op jit(solution)/shard_map/conv_general_dilated | solution.py:46
  1030.5 20.2 %reshape.123 = f32[16,16,1,264,24]{3,4,1,0,2:T(8,128)} reshape(f32[16,16,8,33,24]{3,2,4,1,0:T(8,128)} %copy.174) | data formatting | bytes 12976128 | tf_op jit(solution)/shard_map/conv_general_dilated | solution.py:46
  (107 shorter events, 274.3 us)
Async XLA Ops:
  0.0 750.7 %copy-start = (bf16[24,24,3,3,3]{1,0,4,3,2:T(8,128)(2,1)S(1)}, bf16[24,24,3,3,3]{1,0,4,3,2:T(8,128)(2,1)}, u32[]{:S(2)}) copy-start(bf16[24,24,3,3,3]{1,0,4,3,2:T(8,128)(2,1)} %param.12) | copy-start | bytes 93316
  30.4 8.4 copy-start.2
  257.8 99.6 %all-to-all-start = ((f32[32,1,32768]{2,1,0:T(1,128)}), f32[32,1,32768]{2,1,0:T(1,128)}, u32[]{:S(2)}, u32[]{:S(2)}) async-start(f32[32,1,32768]{2,1,0:T(1,128)} %reshape.143), calls=%async_computation | async-start | bytes 8388608 | tf_op jit(solution)/shard_map/all_to_all | solution.py:77
  488.2 16.8 %copy-start.3 = (f32[2,8,8,16,512]{4,1,3,2,0:T(8,128)S(1)}, f32[2,8,8,16,512]{4,1,3,2,0:T(8,128)}, u32[]{:S(2)}) copy-start(f32[2,8,8,16,512]{4,1,3,2,0:T(8,128)} %copy.187) | copy-start | bytes 12582916
  535.4 9.2 collective-permute-start
  541.8 6.9 collective-permute-start.1
  558.9 16.5 %copy-start.8 = (bf16[24,2,3,3,3]{0,1,4,3,2:T(2,128)(2,1)S(1)}, bf16[24,2,3,3,3]{0,1,4,3,2:T(2,128)(2,1)}, u32[]{:S(2)}) copy-start(bf16[24,2,3,3,3]{0,1,4,3,2:T(2,128)(2,1)} %param.10) | copy-start | bytes 7780
  558.9 16.5 %copy-start.9 = (pred[8,33]{0,1:T(8,128)(4,1)S(1)}, pred[8,33]{0,1:T(8,128)(4,1)}, u32[]{:S(2)}) copy-start(pred[8,33]{0,1:T(8,128)(4,1)} %constant.54) | copy-start | bytes 796
  662.5 20.2 %copy-start.4 = (f32[24]{0:T(128)S(1)}, f32[24]{0:T(128)}, u32[]{:S(2)}) copy-start(f32[24]{0:T(128)} %param.11) | copy-start | bytes 292
  686.4 4.5 collective-permute-start.2
  688.3 8.8 collective-permute-start.3
  846.4 20.2 %copy-start.5 = (f32[24]{0:T(128)S(1)}, f32[24]{0:T(128)}, u32[]{:S(2)}) copy-start(f32[24]{0:T(128)} %param.13) | copy-start | bytes 292
  870.3 4.5 collective-permute-start.4
  872.3 8.8 collective-permute-start.5
  905.7 29.2 %copy-start.7 = (bf16[24,24,3,3,3]{1,0,4,3,2:T(8,128)(2,1)S(1)}, bf16[24,24,3,3,3]{1,0,4,3,2:T(8,128)(2,1)}, u32[]{:S(2)}) copy-start(bf16[24,24,3,3,3]{1,0,4,3,2:T(8,128)(2,1)} %param.14) | copy-start | bytes 93316
  1030.5 20.2 %copy-start.6 = (f32[24]{0:T(128)S(1)}, f32[24]{0:T(128)}, u32[]{:S(2)}) copy-start(f32[24]{0:T(128)} %param.15) | copy-start | bytes 292
  1030.5 26.3 %copy-start.1 = (bf16[24,24,3,3,3]{1,0,4,3,2:T(8,128)(2,1)S(1)}, bf16[24,24,3,3,3]{1,0,4,3,2:T(8,128)(2,1)}, u32[]{:S(2)}) copy-start(bf16[24,24,3,3,3]{1,0,4,3,2:T(8,128)(2,1)} %param.12) | copy-start | bytes 93316
